TPU v7x, 128 devices: a whole 4x4x4 slice. The times are simulated.
128 devices in a mesh: dp: 4 (over y), mp: 32 (over x, z, core).
Axes of the slice: x: 4, y: 4, z: 4, core: 2. Of those that a mesh axis runs over, the one named last changes fastest.
Arguments:
- residual_in: bfloat16 [512, 3584], P('dp', 'mp'), may hold values from -6 to 6
- pre_gain: float32 [3584], replicated, may hold values from 0.5 to 1.5
- post_gain: float32 [3584], replicated, may hold values from 0.5 to 1.5
- w_gate: bfloat16 [3584, 14336], P(None, 'mp'), may hold values from -0.09375 to 0.09375
- w_up: bfloat16 [3584, 14336], P(None, 'mp'), may hold values from -0.09375 to 0.09375
- w_down: bfloat16 [14336, 3584], P('mp'), may hold values from -0.046875 to 0.046875
- w_enc: bfloat16 [3584, 65536], P(None, ('dp', 'mp')), may hold values from -0.09375 to 0.09375
- b_enc: float32 [65536], P(('dp', 'mp')), may hold values from -2.5 to 2.5
- threshold: float32 [65536], P(('dp', 'mp')), may hold values from 0.1 to 1
- w_dec: bfloat16 [65536, 3584], P(('dp', 'mp')), may hold values from -0.0234375 to 0.0234375
- b_dec: float32 [3584], replicated, may hold values from -1.5 to 1.5
Outputs:
- loss_value: float32 [], replicated
- d_w_enc: bfloat16 [3584, 65536], P(None, ('dp', 'mp'))
- d_w_dec: bfloat16 [65536, 3584], P(('dp', 'mp'))
- d_b_enc: float32 [65536], P(('dp', 'mp'))
- d_threshold: float32 [65536], P(('dp', 'mp'))
- d_b_dec: float32 [3584], replicated
All inputs are finite; a program needn't handle non-finite values.
Results may differ from a plain program's by a relative error of at most 0.014.
The roundings to bfloat16 on the way count: a program that leaves them out, or rounds other values in their place, can miss the bound.
Values may be sent and summed in bfloat16 or wider, within the bound.
A program may use at most 128 MiB of HBM per device.

v0:
```python
import jax
import jax.numpy as jnp
from jax import lax
from jax.sharding import PartitionSpec as P

norm_eps = 1e-06
gate_band = 0.1
sparsity_coef = 0.05


def contract_first(left, right):
    return lax.dot_general(
        left, right, (((0,), (0,)), ((), ())), preferred_element_type=jnp.float32
    )


def local(
    residual_in, pre_gain, post_gain, w_gate, w_up, w_down, w_enc, b_enc, threshold, w_dec, b_dec
):
    full_rows = lax.all_gather(residual_in, "mp", axis=1, tiled=True)
    resid_wide = full_rows.astype(jnp.float32)
    normed = (
        resid_wide
        * lax.rsqrt(jnp.mean(resid_wide * resid_wide, axis=1, keepdims=True) + norm_eps)
        * pre_gain[None, :]
    ).astype(jnp.bfloat16)
    gate_out = jnp.dot(normed, w_gate, preferred_element_type=jnp.float32)
    up_out = jnp.dot(normed, w_up, preferred_element_type=jnp.float32)
    hidden = (jax.nn.gelu(gate_out, approximate=True) * up_out).astype(jnp.bfloat16)
    col_width = residual_in.shape[1]
    model_width = full_rows.shape[1]
    out_share = lax.psum_scatter(
        lax.dot_general(
            w_down, hidden, (((0,), (1,)), ((), ())), preferred_element_type=jnp.float32
        ),
        "mp",
        scatter_dimension=0,
        tiled=True,
    )
    total_sq = lax.psum(jnp.sum(out_share * out_share, axis=0), "mp")
    row_scale = lax.rsqrt(total_sq / model_width + norm_eps)
    my_cols = lax.axis_index("mp") * col_width
    gain_share = lax.dynamic_slice_in_dim(post_gain, my_cols, col_width, 0)
    mixed = residual_in.T.astype(jnp.float32) + out_share * row_scale[None, :] * gain_share[:, None]
    column_rows = lax.all_gather(mixed.astype(jnp.bfloat16), "mp", axis=0, tiled=True)
    h_cols = lax.all_gather(column_rows, "dp", axis=1, tiled=True)
    pre_act = contract_first(h_cols, w_enc) + b_enc[None, :]
    soft = jax.nn.sigmoid((pre_act - threshold[None, :]) / gate_band)
    feat_bf = (pre_act * soft).astype(jnp.bfloat16)
    gate_part = jnp.sum(soft)
    recon_part = lax.dot_general(
        w_dec, feat_bf, (((0,), (1,)), ((), ())), preferred_element_type=jnp.float32
    )
    recon_all, gate_total = lax.psum((recon_part, gate_part), ("dp", "mp"))
    error_t = recon_all + b_dec[:, None] - h_cols.astype(jnp.float32)
    grad_bdec = jnp.sum(error_t, axis=1)
    square_total = jnp.sum(error_t * error_t)
    err_bf = error_t.astype(jnp.bfloat16)
    loss_value = (0.5 * square_total + sparsity_coef * gate_total) / (
        h_cols.shape[0] * h_cols.shape[1]
    )
    grad_wdec = lax.dot_general(
        feat_bf, err_bf, (((0,), (1,)), ((), ())), preferred_element_type=jnp.float32
    ).astype(jnp.bfloat16)
    grad_feat = lax.dot_general(
        err_bf, w_dec, (((0,), (1,)), ((), ())), preferred_element_type=jnp.float32
    )
    slope = soft * (1.0 - soft) / gate_band
    side_term = (grad_feat * pre_act + sparsity_coef) * slope
    grad_pre = grad_feat * soft + side_term
    grad_thresh = -jnp.sum(side_term, axis=0)
    grad_benc = jnp.sum(grad_pre, axis=0)
    grad_wenc = jnp.dot(
        h_cols, grad_pre.astype(jnp.bfloat16), preferred_element_type=jnp.float32
    ).astype(jnp.bfloat16)
    return (loss_value, grad_wenc, grad_wdec, grad_benc, grad_thresh, grad_bdec)


def solution(mesh):
    placed = (
        P("dp", "mp"),
        P(),
        P(),
        P(None, "mp"),
        P(None, "mp"),
        P("mp", None),
        P(None, ("dp", "mp")),
        P(("dp", "mp")),
        P(("dp", "mp")),
        P(("dp", "mp"), None),
        P(),
    )
    return jax.shard_map(
        local,
        mesh=mesh,
        in_specs=placed,
        out_specs=(
            P(),
            P(None, ("dp", "mp")),
            P(("dp", "mp"), None),
            P(("dp", "mp")),
            P(("dp", "mp")),
            P(),
        ),
        check_vma=False,
    )
```

profile of v0, /device:TPU:1, one launch (start us, length us, event | category | flops | bytes accessed | tf_op | source)
XLA Modules:
  0.0 526.1 jit_solution(124205612583446622)
XLA Ops:
  7.2 0.0 copy-start
  7.2 0.0 reduce-scatter.4.cloned.1.call-start
  7.2 27.9 %all_gather.9 = bf16[128,3584]{0,1:T(8,128)(2,1)S(1)} all-gather(bf16[128,112]{0,1:T(8,128)(2,1)} %param.11), channel_id=1, replica_groups=mesh['dp'=4,'mp'=32] {'mp'}, dimensions={1}, use_global_device_ids=true | all-gather | bytes 946176 | tf_op jit(solution)/shard_map/all_gather | solution.py:20
  35.1 0.5 fusion.2
  35.6 0.4 copy-done.1
  36.0 3.1 fusion.20
  39.1 6.0 %convolution_bitcast_fusion.1 = f32[3584,128]{0,1:T(8,128)} fusion(bf16[448,3584]{1,0:T(8,128)(2,1)S(1)} %copy-done, f32[128,448]{0,1:T(8,128)S(1)} %fusion.20, bf16[3584,448]{0,1:T(8,128)(2,1)} %param.15, bf16[128,3584]{0,1:T(8,128)(2,1)} %copy-done.1, f32[3584]{0:T(1024)S(1)} %copy-done.3, f32[128]{0:T(128)S(1)} %add_rsqrt_fusion.1), kind=kOutput, calls=%fused_computation.5 | convolution fusion | flops 824033280 | bytes 9419264 | tf_op jit(solution)/shard_map/dot_general | solution.py:33
  45.1 2.7 copy.23
  47.8 0.0 reduce-scatter.4.cloned.1.call-update
  47.8 0.0 all-gather.2.cloned.1.call-start
  47.9 0.8 dynamic_slice.3
  48.6 75.3 %reduce-scatter.4.cloned.1.call-done = f32[112,128]{1,0:T(8,128)} async-done(((f32[3584,128]{1,0:T(8,128)}), f32[112,128]{1,0:T(8,128)}) %reduce-scatter.4.cloned.1.call-update) | async-done | bytes 57360 | tf_op jit(solution)/shard_map/reduce_scatter | solution.py:32
  123.9 0.9 copy.24
  124.8 0.1 multiply_reduce_fusion.1
  124.9 64.3 %psum.21 = f32[128]{0:T(128)S(1)} all-reduce(f32[128]{0:T(128)S(1)} %multiply_reduce_fusion.1), channel_id=1, replica_groups=mesh['dp'=4,'mp'=32] {'mp'}, use_global_device_ids=true, to_apply=%region_3.0 | all-reduce | flops 128 | bytes 1024 | tf_op jit(solution)/shard_map/psum | solution.py:40
  189.3 0.9 fusion.23
  190.2 25.7 %all_gather.10 = bf16[3584,128]{1,0:T(8,128)(2,1)} all-gather(bf16[112,128]{1,0:T(8,128)(2,1)S(1)} %fusion.23), channel_id=1, replica_groups=mesh['dp'=4,'mp'=32] {'mp'}, dimensions={0}, use_global_device_ids=true | all-gather | bytes 946176 | tf_op jit(solution)/shard_map/all_gather | solution.py:45
  215.9 2.2 copy.22
  218.1 0.0 all-gather.2.cloned.1.call-update
  218.1 0.2 all-reduce.2.cloned.1.call-start
  218.3 42.6 %all-gather.2.cloned.1.call-done = bf16[3584,512]{0,1:T(8,128)(2,1)} async-done(((bf16[3584,128]{0,1:T(8,128)(2,1)}), bf16[3584,512]{0,1:T(8,128)(2,1)}) %all-gather.2.cloned.1.call-update) | async-done | bytes 3670032 | tf_op jit(solution)/shard_map/all_gather | solution.py:46
  260.9 5.3 %convolution_add_fusion = f32[512,512]{1,0:T(8,128)S(1)} fusion(bf16[3584,512]{0,1:T(8,128)(2,1)} %all-gather.2.cloned.1.call-done, bf16[3584,512]{1,0:T(8,128)(2,1)} %param.17, f32[512]{0:T(512)S(1)} %copy-done.7), kind=kOutput, calls=%fused_computation.14 | convolution fusion | flops 1879310336 | bytes 8390656 | tf_op jit(solution)/shard_map/dot_general | solution.py:12
  266.3 1.0 copy-done.9
  267.2 5.1 convolution_bitcast_fusion
  272.4 0.0 all-reduce.2.cloned.1.call-update
  272.4 160.2 %all-reduce.2.cloned.1.call-done = f32[3584,512]{0,1:T(8,128)} async-done(((f32[3584,512]{0,1:T(8,128)}), f32[3584,512]{0,1:T(8,128)}) %all-reduce.2.cloned.1.call-update) | async-done | bytes 7340048 | tf_op jit(solution)/shard_map/psum | solution.py:54
  432.6 5.9 %fusion = (f32[3584]{0:T(1024)}, f32[]{:T(128)}, bf16[3584,512]{0,1:T(8,128)(2,1)S(1)}) fusion(bf16[3584,512]{0,1:T(8,128)(2,1)} %all-gather.2.cloned.1.call-done, f32[3584,512]{0,1:T(8,128)} %all-reduce.2.cloned.1.call-done, f32[3584]{0:T(1024)S(1)} %copy-done.4), kind=kLoop, calls=%fused_computation.8 | loop fusion | flops 12841471 | bytes 14708740 | tf_op jit(solution)/shard_map/reduce_sum | solution.py:56
  438.6 3.9 fusion.25
  442.4 4.0 convolution_convert_fusion
  446.4 64.1 %psum.23 = f32[]{:T(128)} all-reduce(f32[]{:T(128)} %get-tuple-element.13), channel_id=1, replica_groups=mesh['dp'=4,'mp'=32] {'dp','mp'}, use_global_device_ids=true, to_apply=%region_7.0 | all-reduce | flops 1 | bytes 8 | tf_op jit(solution)/shard_map/psum | solution.py:54
  510.5 0.6 neg.7
  512.4 6.1 %convolution_convert_fusion.1 = bf16[3584,512]{1,0:T(8,128)(2,1)} fusion(bf16[3584,512]{0,1:T(8,128)(2,1)} %all-gather.2.cloned.1.call-done, bf16[512,512]{1,0:T(8,128)(2,1)} %get-tuple-element.11), kind=kOutput, calls=%fused_computation.4 | convolution fusion | flops 1880883200 | bytes 7864320 | tf_op jit(solution)/shard_map/dot_general | solution.py:73
  (21 shorter events, 0.1 us)
Async XLA Ops:
  7.2 31.9 %copy-start = (bf16[448,3584]{1,0:T(8,128)(2,1)S(1)}, bf16[448,3584]{1,0:T(8,128)(2,1)}, u32[]{:S(2)}) copy-start(bf16[448,3584]{1,0:T(8,128)(2,1)} %param.16) | copy-start | bytes 9633796
  7.2 116.7 %reduce-scatter.4.cloned.1.call-start = ((), (), s32[]{:S(2)}) async-start(), calls=%async_computation.3 | async-start | bytes 1892352 | tf_op jit(solution)/shard_map/reduce_scatter | solution.py:32
  35.1 0.9 copy-start.1
  35.1 4.0 copy-start.3
  45.1 144.2 %copy-start.2 = (bf16[128,112]{0,1:T(8,128)(2,1)S(1)}, bf16[128,112]{0,1:T(8,128)(2,1)}, u32[]{:S(2)}) copy-start(bf16[128,112]{0,1:T(8,128)(2,1)} %param.11) | copy-start | bytes 86020
  47.8 213.1 %copy-start.7 = (f32[512]{0:T(512)S(1)}, f32[512]{0:T(512)}, u32[]{:S(2)}) copy-start(f32[512]{0:T(512)} %param.18) | copy-start | bytes 6148
  47.8 213.1 %all-gather.2.cloned.1.call-start = ((), (), s32[]{:S(2)}) async-start(), calls=%async_computation.1 | async-start | bytes 4587520 | tf_op jit(solution)/shard_map/all_gather | solution.py:46
  218.1 49.1 %copy-start.8 = (f32[512]{0:T(512)S(1)}, f32[512]{0:T(512)}, u32[]{:S(2)}) copy-start(f32[512]{0:T(512)} %param.19) | copy-start | bytes 6148
  218.1 214.5 %all-reduce.2.cloned.1.call-start = ((), (), s32[]{:S(2)}) async-start(), calls=%async_computation.2 | async-start | bytes 14680064 | tf_op jit(solution)/shard_map/psum | solution.py:54
  260.9 6.3 %copy-start.5 = (bf16[512,3584]{1,0:T(8,128)(2,1)S(1)}, bf16[512,3584]{1,0:T(8,128)(2,1)}, u32[]{:S(2)}) copy-start(bf16[512,3584]{1,0:T(8,128)(2,1)} %param.20) | copy-start | bytes 11010052
  266.3 1.0 copy-start.9
  272.4 160.2 %copy-start.4 = (f32[3584]{0:T(1024)S(1)}, f32[3584]{0:T(1024)}, u32[]{:S(2)}) copy-start(f32[3584]{0:T(1024)} %param.21) | copy-start | bytes 43012
  432.6 6.0 %copy-start.6 = (bf16[512,3584]{1,0:T(8,128)(2,1)S(1)}, bf16[512,3584]{1,0:T(8,128)(2,1)}, u32[]{:S(2)}) copy-start(bf16[512,3584]{1,0:T(8,128)(2,1)} %param.20) | copy-start | bytes 11010052
  432.6 6.0 %copy-start.10 = (f32[512,512]{1,0:T(8,128)S(1)}, f32[512,512]{1,0:T(8,128)}, u32[]{:S(2)}) copy-start(f32[512,512]{1,0:T(8,128)} %copy-done.9) | copy-start | bytes 3145732
Sparse Core Ops, SparseCore 0:
  47.9 75.9 reduce-scatter.3
  218.2 42.6 all-gather.1
  272.5 160.0 all-reduce.1
where the time goes:
time: 527 us; the launch traced here: 526 us
  waiting for transfers between devices  278 us (53%)
  blocking collectives  182 us (35%)
  matrix products  33.4 us (6%)
  between operations  16.3 us (3%)
  local copies, waits for them, and re-layouts  8.05 us (2%)
  other arithmetic  8.04 us (2%)
    psum x1, waiting for transfers between devices, local(): recon_all, gate_total = lax.psum((recon_part, gate_part), ('dp', 'mp'))  160 us
    reduce_scatter x1, waiting for transfers between devices, local(): lax.psum_scatter(lax.dot_general(w_down, hidden, (((0,), (1,)), ((), ()))...  75.3 us
    psum x1, blocking collectives, local(): total_sq = lax.psum(jnp.sum(out_share * out_share, axis=0), 'mp')  64.3 us
    psum x1, blocking collectives, local(): recon_all, gate_total = lax.psum((recon_part, gate_part), ('dp', 'mp'))  64.1 us
    all_gather x1, waiting for transfers between devices, local(): h_cols = lax.all_gather(column_rows, 'dp', axis=1, tiled=True)  42.6 us
    all_gather x1, blocking collectives, local(): full_rows = lax.all_gather(residual_in, 'mp', axis=1, tiled=True)  27.9 us
    all_gather x1, blocking collectives, local(): lax.all_gather(mixed.astype(jnp.bfloat16), 'mp', axis=0, tiled=True)  25.7 us
  transfers between devices with their start and end apart: 3, of which 3 were waited for; matrix products, arithmetic and copies ran while one was open for 0% of the time, Pallas kernels for 0%

commit v1 on v0

--- a/solution.py
+++ b/solution.py
@@ -37,7 +37,7 @@
         scatter_dimension=0,
         tiled=True,
     )
-    total_sq = lax.psum(jnp.sum(out_share * out_share, axis=0), "mp")
+    total_sq = jnp.sum(lax.all_gather(jnp.sum(out_share * out_share, axis=0), "mp"), axis=0)
     row_scale = lax.rsqrt(total_sq / model_width + norm_eps)
     my_cols = lax.axis_index("mp") * col_width
     gain_share = lax.dynamic_slice_in_dim(post_gain, my_cols, col_width, 0)

time: 527 us -> 485 us (0.920)
  blocking collectives: 182 us -> 140 us
    psum x1 -> x0, blocking collectives: 64.3 us -> none  [local(): total_sq = lax.psum(jnp.sum(out_share * out_share, axis=0), 'mp')]
    all_gather x0 -> x1, blocking collectives: none -> 22.6 us  [local(): lax.all_gather(jnp.sum(out_share * out_share, axis=0), 'mp')]
where the time goes in v1:
time: 485 us; the launch traced here: 484 us
  waiting for transfers between devices  278 us (57%)
  blocking collectives  140 us (29%)
  matrix products  33.4 us (7%)
  between operations  16.3 us (3%)
  other arithmetic  8.09 us (2%)
  local copies, waits for them, and re-layouts  8.05 us (2%)
    psum x1, waiting for transfers between devices, local(): recon_all, gate_total = lax.psum((recon_part, gate_part), ('dp', 'mp'))  160 us
    reduce_scatter x1, waiting for transfers between devices, local(): lax.psum_scatter(lax.dot_general(w_down, hidden, (((0,), (1,)), ((), ()))...  75.3 us
    psum x1, blocking collectives, local(): recon_all, gate_total = lax.psum((recon_part, gate_part), ('dp', 'mp'))  64.1 us
    all_gather x1, waiting for transfers between devices, local(): h_cols = lax.all_gather(column_rows, 'dp', axis=1, tiled=True)  43 us
    all_gather x1, blocking collectives, local(): full_rows = lax.all_gather(residual_in, 'mp', axis=1, tiled=True)  27.9 us
    all_gather x1, blocking collectives, local(): lax.all_gather(mixed.astype(jnp.bfloat16), 'mp', axis=0, tiled=True)  25.2 us
    all_gather x1, blocking collectives, local(): lax.all_gather(jnp.sum(out_share * out_share, axis=0), 'mp')  22.6 us
  transfers between devices with their start and end apart: 3, of which 3 were waited for; matrix products, arithmetic and copies ran while one was open for 0% of the time, Pallas kernels for 0%

profile of v1, /device:TPU:1, one launch (start us, length us, event | category | flops | bytes accessed | tf_op | source)
XLA Modules:
  0.0 484.2 jit_solution(3020985249148445307)
XLA Ops:
  7.2 0.0 reduce-scatter.4.cloned.1.call-start
  7.2 27.9 %all_gather.15 = bf16[128,3584]{0,1:T(8,128)(2,1)S(1)} all-gather(bf16[128,112]{0,1:T(8,128)(2,1)} %param.11), channel_id=1, replica_groups=mesh['dp'=4,'mp'=32] {'mp'}, dimensions={1}, use_global_device_ids=true | all-gather | bytes 946176 | tf_op jit(solution)/shard_map/all_gather | solution.py:20
  35.1 0.5 fusion.2
  35.6 0.4 copy-done.1
  36.0 3.1 fusion.20
  39.1 6.0 %convolution_bitcast_fusion.1 = f32[3584,128]{0,1:T(8,128)} fusion(bf16[448,3584]{1,0:T(8,128)(2,1)S(1)} %copy-done, f32[128,448]{0,1:T(8,128)S(1)} %fusion.20, bf16[3584,448]{0,1:T(8,128)(2,1)} %param.15, bf16[128,3584]{0,1:T(8,128)(2,1)} %copy-done.1, f32[3584]{0:T(1024)S(1)} %copy-done.3, f32[128]{0:T(128)S(1)} %add_rsqrt_fusion.1), kind=kOutput, calls=%fused_computation.5 | convolution fusion | flops 824033280 | bytes 9419264 | tf_op jit(solution)/shard_map/dot_general | solution.py:33
  45.1 2.7 copy.23
  47.8 0.0 reduce-scatter.4.cloned.1.call-update
  47.8 0.0 all-gather.4.cloned.1.call-start
  47.9 0.8 dynamic_slice.3
  48.6 75.3 %reduce-scatter.4.cloned.1.call-done = f32[112,128]{1,0:T(8,128)} async-done(((f32[3584,128]{1,0:T(8,128)}), f32[112,128]{1,0:T(8,128)}) %reduce-scatter.4.cloned.1.call-update) | async-done | bytes 57360 | tf_op jit(solution)/shard_map/reduce_scatter | solution.py:32
  123.9 0.9 copy.24
  124.8 0.1 multiply_reduce_fusion.1
  124.9 22.6 %all-gather.1 = f32[32,1,128]{2,1,0:T(1,128)S(1)} all-gather(f32[1,1,128]{2,1,0:T(1,128)S(1)} %bitcast.21), channel_id=2, replica_groups=mesh['dp'=4,'mp'=32] {'mp'}, dimensions={0}, use_global_device_ids=true | all-gather | bytes 16896 | tf_op jit(solution)/shard_map/all_gather | solution.py:40
  147.5 0.1 reduce_sum.74
  147.6 0.9 fusion.23
  148.5 25.2 %all_gather.18 = bf16[3584,128]{1,0:T(8,128)(2,1)} all-gather(bf16[112,128]{1,0:T(8,128)(2,1)S(1)} %fusion.23), channel_id=1, replica_groups=mesh['dp'=4,'mp'=32] {'mp'}, dimensions={0}, use_global_device_ids=true | all-gather | bytes 946176 | tf_op jit(solution)/shard_map/all_gather | solution.py:45
  173.7 2.2 copy.22
  175.9 0.0 all-gather.4.cloned.1.call-update
  175.9 0.2 all-reduce.2.cloned.1.call-start
  176.1 43.0 %all-gather.4.cloned.1.call-done = bf16[3584,512]{0,1:T(8,128)(2,1)} async-done(((bf16[3584,128]{0,1:T(8,128)(2,1)}), bf16[3584,512]{0,1:T(8,128)(2,1)}) %all-gather.4.cloned.1.call-update) | async-done | bytes 3670032 | tf_op jit(solution)/shard_map/all_gather | solution.py:46
  219.1 5.3 %convolution_add_fusion = f32[512,512]{1,0:T(8,128)S(1)} fusion(bf16[3584,512]{0,1:T(8,128)(2,1)} %all-gather.4.cloned.1.call-done, bf16[3584,512]{1,0:T(8,128)(2,1)} %param.17, f32[512]{0:T(512)S(1)} %copy-done.7), kind=kOutput, calls=%fused_computation.14 | convolution fusion | flops 1879310336 | bytes 8390656 | tf_op jit(solution)/shard_map/dot_general | solution.py:12
  224.5 1.0 copy-done.9
  225.5 5.2 %convolution_bitcast_fusion = f32[3584,512]{0,1:T(8,128)} fusion(bf16[512,3584]{1,0:T(8,128)(2,1)S(1)} %copy-done.5, f32[512,512]{1,0:T(8,128)S(1)} %convolution_add_fusion, f32[512]{0:T(512)S(1)} %copy-done.8), kind=kOutput, calls=%fused_computation.2 | convolution fusion | flops 1880883200 | bytes 12060672 | tf_op jit(solution)/shard_map/dot_general | solution.py:51
  230.6 0.0 all-reduce.2.cloned.1.call-update
  230.6 160.1 %all-reduce.2.cloned.1.call-done = f32[3584,512]{0,1:T(8,128)} async-done(((f32[3584,512]{0,1:T(8,128)}), f32[3584,512]{0,1:T(8,128)}) %all-reduce.2.cloned.1.call-update) | async-done | bytes 7340048 | tf_op jit(solution)/shard_map/psum | solution.py:54
  390.8 5.9 %fusion = (f32[3584]{0:T(1024)}, f32[]{:T(128)}, bf16[3584,512]{0,1:T(8,128)(2,1)S(1)}) fusion(bf16[3584,512]{0,1:T(8,128)(2,1)} %all-gather.4.cloned.1.call-done, f32[3584,512]{0,1:T(8,128)} %all-reduce.2.cloned.1.call-done, f32[3584]{0:T(1024)S(1)} %copy-done.4), kind=kLoop, calls=%fused_computation.8 | loop fusion | flops 12841471 | bytes 14708740 | tf_op jit(solution)/shard_map/reduce_sum | solution.py:56
  396.7 3.9 fusion.25
  400.6 4.0 convolution_convert_fusion
  404.6 64.1 %psum.15 = f32[]{:T(128)} all-reduce(f32[]{:T(128)} %get-tuple-element.13), channel_id=1, replica_groups=mesh['dp'=4,'mp'=32] {'dp','mp'}, use_global_device_ids=true, to_apply=%region_7.0 | all-reduce | flops 1 | bytes 8 | tf_op jit(solution)/shard_map/psum | solution.py:54
  468.6 0.6 neg.7
  470.5 6.1 %convolution_convert_fusion.1 = bf16[3584,512]{1,0:T(8,128)(2,1)} fusion(bf16[3584,512]{0,1:T(8,128)(2,1)} %all-gather.4.cloned.1.call-done, bf16[512,512]{1,0:T(8,128)(2,1)} %get-tuple-element.11), kind=kOutput, calls=%fused_computation.4 | convolution fusion | flops 1880883200 | bytes 7864320 | tf_op jit(solution)/shard_map/dot_general | solution.py:73
  (22 shorter events, 0.1 us)
Async XLA Ops:
  7.2 31.9 %copy-start = (bf16[448,3584]{1,0:T(8,128)(2,1)S(1)}, bf16[448,3584]{1,0:T(8,128)(2,1)}, u32[]{:S(2)}) copy-start(bf16[448,3584]{1,0:T(8,128)(2,1)} %param.16) | copy-start | bytes 9633796
  7.2 116.7 %reduce-scatter.4.cloned.1.call-start = ((), (), s32[]{:S(2)}) async-start(), calls=%async_computation.3 | async-start | bytes 1892352 | tf_op jit(solution)/shard_map/reduce_scatter | solution.py:32
  35.1 0.9 copy-start.1
  35.1 4.0 copy-start.3
  45.1 102.5 %copy-start.2 = (bf16[128,112]{0,1:T(8,128)(2,1)S(1)}, bf16[128,112]{0,1:T(8,128)(2,1)}, u32[]{:S(2)}) copy-start(bf16[128,112]{0,1:T(8,128)(2,1)} %param.11) | copy-start | bytes 86020
  47.8 171.3 %copy-start.7 = (f32[512]{0:T(512)S(1)}, f32[512]{0:T(512)}, u32[]{:S(2)}) copy-start(f32[512]{0:T(512)} %param.18) | copy-start | bytes 6148
  47.8 171.3 %all-gather.4.cloned.1.call-start = ((), (), s32[]{:S(2)}) async-start(), calls=%async_computation.1 | async-start | bytes 4587520 | tf_op jit(solution)/shard_map/all_gather | solution.py:46
  175.9 49.5 %copy-start.8 = (f32[512]{0:T(512)S(1)}, f32[512]{0:T(512)}, u32[]{:S(2)}) copy-start(f32[512]{0:T(512)} %param.19) | copy-start | bytes 6148
  175.9 214.8 %all-reduce.2.cloned.1.call-start = ((), (), s32[]{:S(2)}) async-start(), calls=%async_computation.2 | async-start | bytes 14680064 | tf_op jit(solution)/shard_map/psum | solution.py:54
  219.1 6.3 %copy-start.5 = (bf16[512,3584]{1,0:T(8,128)(2,1)S(1)}, bf16[512,3584]{1,0:T(8,128)(2,1)}, u32[]{:S(2)}) copy-start(bf16[512,3584]{1,0:T(8,128)(2,1)} %param.20) | copy-start | bytes 11010052
  224.5 1.0 copy-start.9
  230.6 160.1 %copy-start.4 = (f32[3584]{0:T(1024)S(1)}, f32[3584]{0:T(1024)}, u32[]{:S(2)}) copy-start(f32[3584]{0:T(1024)} %param.21) | copy-start | bytes 43012
  390.8 6.0 %copy-start.6 = (bf16[512,3584]{1,0:T(8,128)(2,1)S(1)}, bf16[512,3584]{1,0:T(8,128)(2,1)}, u32[]{:S(2)}) copy-start(bf16[512,3584]{1,0:T(8,128)(2,1)} %param.20) | copy-start | bytes 11010052
  390.8 6.0 %copy-start.10 = (f32[512,512]{1,0:T(8,128)S(1)}, f32[512,512]{1,0:T(8,128)}, u32[]{:S(2)}) copy-start(f32[512,512]{1,0:T(8,128)} %copy-done.9) | copy-start | bytes 3145732
Sparse Core Ops, SparseCore 0:
  47.9 75.9 reduce-scatter.3
  176.0 43.0 all-gather.3
  230.8 159.9 all-reduce.1
